TPU v7x, 512 devices: a whole 4x4x16 slice. The times are simulated.
512 devices in a mesh: dp: 8 (over z_lo, core), expert: 64 (over x, z_hi, y).
Axes of the slice: x: 4, y: 4, z: 16 (z_hi: 4, z_lo: 4; z = z_hi * 4 + z_lo), core: 2. Of those that a mesh axis runs over, the one named last changes fastest.
Arguments:
- grad_out: bfloat16 [16384, 2048], P(('dp', 'expert')), may hold values from -6 to 6
- hidden: bfloat16 [16384, 8, 768], P(('dp', 'expert')), may hold values from -0.29882812 to 0.29882812
- gates: bfloat16 [16384, 8], P(('dp', 'expert')), may hold values from 0.049804688 to 1
- routes: int32 [16384, 8], P(('dp', 'expert')), may hold values from 0 to 63, as said below
- weights: bfloat16 [64, 768, 2048], P('expert'), may hold values from -0.125 to 0.125
Outputs:
- hidden_grad: bfloat16 [16384, 8, 768], P(('dp', 'expert'))
- gate_grad: float32 [16384, 8], P(('dp', 'expert'))
- weight_grad: float32 [64, 768, 2048], P('expert', 'dp')
Inputs may be any that keep to these rules, and one draw needn't show every extreme that they name: `routes`: each row names 8 different experts. In each aligned block of 32 rows (the rows of one device) no expert is named more than 12 times, and some expert is named exactly 12 times in every block.
All inputs are finite; a program needn't handle non-finite values.
Results may differ from a plain program's by a relative error of at most 0.015.
Values may be sent and summed in bfloat16 or wider, within the bound.
A program may use at most 128 MiB of HBM per device.

v0:
```python
import jax
import jax.numpy as jnp
from jax import lax
from jax.sharding import PartitionSpec as P


def project(rows_in, matrix):
    return lax.dot_general(
        rows_in, matrix, (((1,), (1,)), ((), ())), preferred_element_type=jnp.float32
    ).astype(jnp.bfloat16)


def outer_slab(hidden_rows, scaled_rows):
    return lax.dot_general(
        hidden_rows, scaled_rows, (((0,), (0,)), ((), ())), preferred_element_type=jnp.float32
    )


def on_device(grad_out, hidden, gates, routes, weights):
    tokens, picks_each = routes.shape
    model_width = grad_out.shape[1]
    hidden_width = hidden.shape[2]
    experts = lax.axis_size("expert")
    capacity = max(2, min(tokens, 3 * tokens * picks_each // experts))
    slot_total = experts * capacity
    expert_ids = jnp.arange(experts, dtype=jnp.int32)
    route_list = routes.reshape(-1)
    onehot = (route_list[:, None] == expert_ids[None, :]).astype(jnp.int32)
    slot_ranks = jnp.cumsum(onehot, axis=0) - 1
    slot_index = route_list * capacity + jnp.sum(slot_ranks * onehot, axis=1)
    grad_rows = jnp.repeat(grad_out, picks_each, axis=0)
    hidden_rows = hidden.reshape(tokens * picks_each, hidden_width)
    gate_list = gates.reshape(-1)
    send_grad = jnp.zeros((slot_total, model_width), jnp.bfloat16).at[slot_index].set(grad_rows)
    send_hidden = (
        jnp.zeros((slot_total, hidden_width), jnp.bfloat16).at[slot_index].set(hidden_rows)
    )
    send_gate = jnp.zeros((slot_total,), jnp.bfloat16).at[slot_index].set(gate_list)
    got_grad, got_hidden, got_gate = (
        lax.all_to_all(
            send_grad.reshape(experts, capacity, model_width),
            "expert",
            split_axis=0,
            concat_axis=0,
            tiled=True,
        ),
        lax.all_to_all(
            send_hidden.reshape(experts, capacity, hidden_width),
            "expert",
            split_axis=0,
            concat_axis=0,
            tiled=True,
        ),
        lax.all_to_all(
            send_gate.reshape(experts, capacity), "expert", split_axis=0, concat_axis=0, tiled=True
        ),
    )
    owner_grad = got_grad.reshape(slot_total, model_width)
    owner_hidden = got_hidden.reshape(slot_total, hidden_width)
    owner_gate = got_gate.reshape(slot_total)
    owner_scaled = (
        owner_gate.astype(jnp.float32)[:, None] * owner_grad.astype(jnp.float32)
    ).astype(jnp.bfloat16)
    matrix = weights[0]
    proj_rows = project(owner_grad, matrix)
    returned = lax.all_to_all(
        proj_rows.reshape(experts, capacity, hidden_width),
        "expert",
        split_axis=0,
        concat_axis=0,
        tiled=True,
    )
    route_proj = returned.reshape(slot_total, hidden_width)[slot_index]
    gate_float = gate_list.astype(jnp.float32)
    proj_float = route_proj.astype(jnp.float32)
    hidden_grad = (
        (gate_float[:, None] * proj_float)
        .astype(jnp.bfloat16)
        .reshape(tokens, picks_each, hidden_width)
    )
    gate_grad = jnp.sum(proj_float * hidden_rows.astype(jnp.float32), axis=1).reshape(
        tokens, picks_each
    )
    shard_rows = hidden_width // lax.axis_size("dp")
    weight_grad = lax.psum_scatter(
        outer_slab(owner_hidden, owner_scaled).astype(jnp.bfloat16),
        "dp",
        scatter_dimension=0,
        tiled=True,
    ).astype(jnp.float32)
    return (hidden_grad, gate_grad, weight_grad.reshape(1, shard_rows, model_width))


def solution(mesh):
    return jax.shard_map(
        on_device,
        mesh=mesh,
        in_specs=(
            P(("dp", "expert"), None),
            P(("dp", "expert"), None, None),
            P(("dp", "expert"), None),
            P(("dp", "expert"), None),
            P("expert", None, None),
        ),
        out_specs=(
            P(("dp", "expert"), None, None),
            P(("dp", "expert"), None),
            P("expert", "dp", None),
        ),
        check_vma=False,
    )
```

profile of v0, /device:TPU:1, one launch (start us, length us, event | category | flops | bytes accessed | tf_op | source)
XLA Modules:
  0.0 482.3 jit_solution(12052748440561585869)
XLA Ops:
  7.2 0.8 broadcast_multiply_fusion
  8.0 0.9 copy.19
  9.3 0.6 reduce-window.6
  9.9 0.2 slice_reduce_fusion
  10.1 0.8 copy.22
  11.1 2.2 scatter_custom_fusion.2
  13.3 0.7 all_to_all.20
  14.0 22.0 %all-to-all-start.3 = ((bf16[64,1,12]{2,1,0:T(2,128)(2,1)}), bf16[64,1,12]{2,1,0:T(2,128)(2,1)}, u32[]{:S(2)}, u32[]{:S(2)}) async-start(bf16[64,1,12]{2,1,0:T(2,128)(2,1)} %all_to_all.20), calls=%async_computation.3 | async-start | bytes 65536 | tf_op jit(solution)/shard_map/all_to_all | solution.py:54
  36.0 4.7 scatter_custom_fusion
  40.7 6.1 %reshape.123 = bf16[64,12,2048]{2,1,0:T(8,128)(2,1)} reshape(bf16[768,2048]{1,0:T(8,128)(2,1)} %scatter_custom_fusion) | data formatting | bytes 6291456 | tf_op jit(solution)/shard_map/reshape | solution.py:41
  46.7 4.7 all-to-all-done.3
  51.4 12.6 %all-to-all-start = ((bf16[64,12,2048]{2,1,0:T(8,128)(2,1)}), bf16[64,12,2048]{2,1,0:T(8,128)(2,1)}, u32[]{:S(2)}, u32[]{:S(2)}) async-start(bf16[64,12,2048]{2,1,0:T(8,128)(2,1)} %reshape.123), calls=%async_computation | async-start | bytes 8388608 | tf_op jit(solution)/shard_map/all_to_all | solution.py:40
  64.1 2.7 scatter_custom_fusion.1
  66.8 3.1 reshape.128
  69.9 180.0 %all-to-all-done = bf16[64,12,2048]{2,1,0:T(8,128)(2,1)} async-done(((bf16[64,12,2048]{2,1,0:T(8,128)(2,1)}), bf16[64,12,2048]{2,1,0:T(8,128)(2,1)}, u32[]{:S(2)}, u32[]{:S(2)}) %all-to-all-start) | async-done | bytes 3145760 | tf_op jit(solution)/shard_map/all_to_all | solution.py:40
  250.0 12.3 %all-to-all-start.2 = ((bf16[64,12,768]{2,1,0:T(8,128)(2,1)}), bf16[64,12,768]{2,1,0:T(8,128)(2,1)}, u32[]{:S(2)}, u32[]{:S(2)}) async-start(bf16[64,12,768]{2,1,0:T(8,128)(2,1)} %reshape.128), calls=%async_computation.2 | async-start | bytes 3145728 | tf_op jit(solution)/shard_map/all_to_all | solution.py:47
  262.2 0.2 reduce-scatter.2.cloned.1.call-start
  262.5 0.8 convert_element_type.66
  263.3 4.9 %multiply_convert_fusion = bf16[64,12,2048]{2,1,0:T(8,128)(2,1)} fusion(bf16[64,12,2048]{2,1,0:T(8,128)(2,1)} %all-to-all-done, f32[64,12]{1,0:T(8,128)S(1)} %bitcast.39), kind=kLoop, calls=%fused_computation.4 | loop fusion | flops 4718592 | bytes 6294528 | tf_op jit(solution)/shard_map/convert_element_type | solution.py:63
  268.2 68.6 %all-to-all-done.2 = bf16[64,12,768]{2,1,0:T(8,128)(2,1)} async-done(((bf16[64,12,768]{2,1,0:T(8,128)(2,1)}), bf16[64,12,768]{2,1,0:T(8,128)(2,1)}, u32[]{:S(2)}, u32[]{:S(2)}) %all-to-all-start.2) | async-done | bytes 1179680 | tf_op jit(solution)/shard_map/all_to_all | solution.py:47
  336.8 9.9 %bitcast_convert_fusion = bf16[768,2048]{1,0:T(8,128)(2,1)} fusion(bf16[64,12,2048]{2,1,0:T(8,128)(2,1)} %multiply_convert_fusion, bf16[64,12,768]{2,1,0:T(8,128)(2,1)} %all-to-all-done.2), kind=kOutput, calls=%fused_computation.5 | convolution fusion | flops 2417491968 | bytes 7471104 | tf_op jit(solution)/shard_map/dot_general | solution.py:14
  346.7 6.2 %reshape.124 = bf16[768,2048]{1,0:T(8,128)(2,1)} reshape(bf16[64,12,2048]{2,1,0:T(8,128)(2,1)} %all-to-all-done) | data formatting | bytes 6291456 | tf_op jit(solution)/shard_map/reshape | solution.py:58
  352.9 5.5 %fusion.5 = bf16[768,768]{1,0:T(8,128)(2,1)} fusion(bf16[768,2048]{1,0:T(8,128)(2,1)} %reshape.124, bf16[1,768,2048]{2,1,0:T(8,128)(2,1)S(1)} %copy-done), kind=kOutput, calls=%fused_computation.11 | convolution fusion | flops 2416508928 | bytes 7471104 | tf_op jit(solution)/shard_map/dot_general | solution.py:8
  358.5 3.2 reshape.125
  361.6 10.6 %all-to-all-start.1 = ((bf16[64,12,768]{2,1,0:T(8,128)(2,1)}), bf16[64,12,768]{2,1,0:T(8,128)(2,1)}, u32[]{:S(2)}, u32[]{:S(2)}) async-start(bf16[64,12,768]{2,1,0:T(8,128)(2,1)} %reshape.125), calls=%async_computation.1 | async-start | bytes 3145728 | tf_op jit(solution)/shard_map/all_to_all | solution.py:66
  372.2 0.7 copy.17
  372.9 91.3 %all-to-all-done.1 = bf16[64,12,768]{2,1,0:T(8,128)(2,1)} async-done(((bf16[64,12,768]{2,1,0:T(8,128)(2,1)}), bf16[64,12,768]{2,1,0:T(8,128)(2,1)}, u32[]{:S(2)}, u32[]{:S(2)}) %all-to-all-start.1) | async-done | bytes 1179680 | tf_op jit(solution)/shard_map/all_to_all | solution.py:66
  464.2 3.1 reshape.126
  467.4 3.6 gather_fusion
  470.9 1.9 fusion.11
  472.9 0.7 copy.26
  473.5 1.9 bitcast_convert_fusion.1
  (19 shorter events, 0.6 us)
Async XLA Ops:
  7.2 345.8 %copy-start = (bf16[1,768,2048]{2,1,0:T(8,128)(2,1)S(1)}, bf16[1,768,2048]{2,1,0:T(8,128)(2,1)}, u32[]{:S(2)}) copy-start(bf16[1,768,2048]{2,1,0:T(8,128)(2,1)} %param.9) | copy-start | bytes 9437188
  14.0 37.5 %all-to-all-start.3 = ((bf16[64,1,12]{2,1,0:T(2,128)(2,1)}), bf16[64,1,12]{2,1,0:T(2,128)(2,1)}, u32[]{:S(2)}, u32[]{:S(2)}) async-start(bf16[64,1,12]{2,1,0:T(2,128)(2,1)} %all_to_all.20), calls=%async_computation.3 | async-start | bytes 65536 | tf_op jit(solution)/shard_map/all_to_all | solution.py:54
  46.7 17.3 %copy-start.1 = (bf16[32,8,768]{2,1,0:T(8,128)(2,1)S(1)}, bf16[32,8,768]{2,1,0:T(8,128)(2,1)}, u32[]{:S(2)}) copy-start(bf16[32,8,768]{2,1,0:T(8,128)(2,1)} %param.6) | copy-start | bytes 1179652
  51.4 198.5 %all-to-all-start = ((bf16[64,12,2048]{2,1,0:T(8,128)(2,1)}), bf16[64,12,2048]{2,1,0:T(8,128)(2,1)}, u32[]{:S(2)}, u32[]{:S(2)}) async-start(bf16[64,12,2048]{2,1,0:T(8,128)(2,1)} %reshape.123), calls=%async_computation | async-start | bytes 8388608 | tf_op jit(solution)/shard_map/all_to_all | solution.py:40
  250.0 86.9 %all-to-all-start.2 = ((bf16[64,12,768]{2,1,0:T(8,128)(2,1)}), bf16[64,12,768]{2,1,0:T(8,128)(2,1)}, u32[]{:S(2)}, u32[]{:S(2)}) async-start(bf16[64,12,768]{2,1,0:T(8,128)(2,1)} %reshape.128), calls=%async_computation.2 | async-start | bytes 3145728 | tf_op jit(solution)/shard_map/all_to_all | solution.py:47
  262.2 211.3 %reduce-scatter.2.cloned.1.call-start = ((), (), s32[]{:S(2)}) async-start(), calls=%async_computation.5 | async-start | bytes 3538944 | tf_op jit(solution)/shard_map/reduce_scatter | solution.py:85
  358.5 13.8 %copy-start.2 = (bf16[32,8]{0,1:T(8,128)(2,1)S(1)}, bf16[32,8]{0,1:T(8,128)(2,1)}, u32[]{:S(2)}) copy-start(bf16[32,8]{0,1:T(8,128)(2,1)} %param.7) | copy-start | bytes 1540
  361.6 102.6 %all-to-all-start.1 = ((bf16[64,12,768]{2,1,0:T(8,128)(2,1)}), bf16[64,12,768]{2,1,0:T(8,128)(2,1)}, u32[]{:S(2)}, u32[]{:S(2)}) async-start(bf16[64,12,768]{2,1,0:T(8,128)(2,1)} %reshape.125), calls=%async_computation.1 | async-start | bytes 3145728 | tf_op jit(solution)/shard_map/all_to_all | solution.py:66
Sparse Core Ops, SparseCore 0:
  346.9 107.0 reduce-scatter.1
where the time goes:
time: 487 us; the launch traced here: 482 us
  waiting for transfers between devices  345 us (71%)
  starting transfers between devices  57.7 us (12%)
  local copies, waits for them, and re-layouts  39.2 us (8%)
  matrix products  15.4 us (3%)
  between operations  14.1 us (3%)
  other arithmetic  11.2 us (2%)
    all_to_all x1, waiting for transfers between devices, on_device(): lax.all_to_all(send_grad.reshape(experts, capacity, model_width), 'expert...  180 us
    all_to_all x1, waiting for transfers between devices, on_device(): lax.all_to_all(proj_rows.reshape(experts, capacity, hidden_width), 'exper...  91.3 us
    all_to_all x1, waiting for transfers between devices, on_device(): lax.all_to_all(send_hidden.reshape(experts, capacity, hidden_width), 'exp...  68.6 us
    all_to_all x1, starting transfers between devices, on_device(): lax.all_to_all(send_gate.reshape(experts, capacity), 'expert', split_axis...  22 us
    all_to_all x1, starting transfers between devices, on_device(): lax.all_to_all(send_grad.reshape(experts, capacity, model_width), 'expert...  12.6 us
    all_to_all x1, starting transfers between devices, on_device(): lax.all_to_all(send_hidden.reshape(experts, capacity, hidden_width), 'exp...  12.3 us
    all_to_all x1, starting transfers between devices, on_device(): lax.all_to_all(proj_rows.reshape(experts, capacity, hidden_width), 'exper...  10.6 us
    dot_general x1, matrix products, outer_slab(): lax.dot_general(hidden_rows, scaled_rows, (((0,), (0,)), ((), ())), prefe...  9.89 us
  transfers between devices with their start and end apart: 5, of which 4 were waited for; matrix products, arithmetic and copies ran while one was open for 10% of the time, Pallas kernels for 0%

commit v1 on v0

v1 whole, which is shorter than its diff:
```python
import functools

import jax
import jax.numpy as jnp
from jax import lax
from jax.experimental import pallas as pl
from jax.experimental.pallas import tpu as pltpu
from jax.sharding import PartitionSpec as P

MESH = pl.DeviceIdType.MESH
BF = jnp.bfloat16
F32 = jnp.float32
I32 = jnp.int32

TOK = 32
TOP = 8
ROUTES = TOK * TOP
D = 2048
F = 768
CUT = 640
SLOT = 16
PEERS = 32
ROWS = PEERS * SLOT
CH = 16
CR = F // CH
SLAB = 192
SUB = 4
SR = SLAB // SUB


def iota(shape, dim):
    return lax.broadcasted_iota(I32, shape, dim)


def dot(a, b, dims=((1,), (0,))):
    return lax.dot_general(a, b, (dims, ((), ())), preferred_element_type=F32)


def pick(mask):
    return jnp.where(mask, 1.0, 0.0).astype(BF)


def kernel(
    routes_ref, gates_ref, grad_ref, hid_ref, w_ref,
    hg_ref, gg_ref, wg_ref,
    tok, meta, meta_out, pack, got, cell, back, rowsel, colsel, gcol_ref,
    wbuf, g, ht, proj5, part, land_p, land_m, fin_out, fin_in,
    w_sem, meta_s, meta_r, tok_s, tok_r, fwd_s, fwd_r, hid_s, hid_r, ret_s, ret_r,
    rel_s, rel_r, rs_s, rs_rp, rs_rm, fin_s, fin_r,
):
    dp = lax.axis_index("dp")
    ex = lax.axis_index("expert")
    zl, c = dp // 2, dp % 2
    x, zb, y = ex // 16, (ex // 4) % 4, ex % 4
    z = zb * 4 + zl
    side = zb % 2 != c
    home = zb % 2 == c
    up = (z + 1) % 16
    down = (z + 15) % 16

    def plane(j, sign):
        dc, dx, dy = j // 16, (j // 4) % 4, j % 4
        if sign < 0:
            dx, dy = 4 - dx, 4 - dy
        return (zl * 2 + (c + dc) % 2, ((x + dx) % 4) * 16 + zb * 4 + (y + dy) % 4)

    def column(zz):
        return ((zz % 4) * 2 + c, x * 16 + (zz // 4) * 4 + y)

    partner = (zl * 2 + (c + 1) % 2, ex)

    def remote(src, dst, s, r, to):
        return pltpu.make_async_remote_copy(
            src_ref=src, dst_ref=dst, send_sem=s, recv_sem=r, device_id=to, device_id_type=MESH
        )

    def slot_rows(j, n=SLOT):
        return pl.ds(pl.multiple_of(j * n, n), n)

    barrier = pltpu.get_barrier_semaphore()

    def greet(j, carry):
        pl.semaphore_signal(barrier, inc=1, device_id=plane(j, 1), device_id_type=MESH)
        return carry

    lax.fori_loop(1, PEERS, greet, 0)
    pl.semaphore_signal(barrier, inc=1, device_id=column(up), device_id_type=MESH)
    pl.semaphore_signal(barrier, inc=1, device_id=column(down), device_id_type=MESH)

    own_q = zb // 2

    @pl.when(home)
    def _():
        pltpu.make_async_copy(w_ref, wbuf.at[own_q], w_sem).start()

    tok[pl.ds(0, TOK), :] = grad_ref[...]

    routes = routes_ref[...].astype(F32)
    shifted = dot(
        routes.astype(BF), pick(iota((TOK, 512), 1) == (iota((TOK, 512), 0) + (iota((TOK, 512), 1) // 128) * 160))
    )
    for v in range(4):
        meta_out[v] = jnp.concatenate(
            [shifted[:, v * 128 : (v + 1) * 128], jnp.zeros((8, 128), F32)], axis=0
        ).astype(BF)
    meta[0] = meta_out[0]

    pl.semaphore_wait(barrier, PEERS - 1 + 2)

    def send_meta(j, carry):
        remote(meta_out.at[j % 4], meta.at[j], meta_s, meta_r, plane(j, 1)).start()
        return carry

    lax.fori_loop(1, PEERS, send_meta, 0)

    def send_tok(j, carry):
        remote(tok.at[pl.ds(0, TOK)], tok.at[slot_rows(j, TOK)], tok_s, tok_r.at[j], plane(j, 1)).start()
        return carry

    lax.fori_loop(1, 16, send_tok, 0)
    remote(tok.at[pl.ds(0, TOK)], tok.at[pl.ds(16 * TOK, TOK)], tok_s, fwd_r, partner).start()

    def w_rows(i):
        return pl.ds(pl.multiple_of(i * CR, CR), CR)

    def w_copy(q, i, way):
        chunk = i if way == 0 else CH - 1 - i
        return remote(
            wbuf.at[q, w_rows(chunk)], wbuf.at[q, w_rows(chunk)],
            rel_s.at[way, i], rel_r.at[way, i], column(up if way == 0 else down),
        )

    @pl.when(home)
    def _():
        pltpu.make_async_copy(w_ref, wbuf.at[own_q], w_sem).wait()

    for way, edge in ((0, 3), (1, 0)):

        @pl.when(home & (zl == edge))
        def _():
            def start(i, carry):
                w_copy(own_q, i, way).start()
                return carry

            lax.fori_loop(0, CH, start, 0)

    rt = routes.astype(BF)
    widen = pick(iota((TOK, ROUTES), 1) // TOP == iota((TOK, ROUTES), 0))
    keep = iota((TOP, ROUTES), 1) % TOP == iota((TOP, ROUTES), 0)
    route_row = jnp.sum(jnp.where(keep, dot(rt, widen), 0.0), axis=0, keepdims=True)
    gate_row = jnp.sum(jnp.where(keep, dot(gates_ref[...], widen), 0.0), axis=0, keepdims=True)
    member = jnp.zeros((64, TOK), F32)
    for k in range(TOP):
        member += jnp.where(iota((64, TOK), 0) == routes_ref[k : k + 1, :], 1.0, 0.0)
    before = pick(iota((TOK, TOK), 0) < iota((TOK, TOK), 1))
    rank = dot(member.astype(BF), before)
    rank = dot(rank.astype(BF), widen)
    route_int = route_row.astype(I32)
    rank_row = jnp.sum(
        jnp.where(iota((64, ROUTES), 0) == route_int, rank, 0.0), axis=0, keepdims=True
    ).astype(I32)
    xe, ze, ye = route_int >> 4, (route_int >> 2) & 3, route_int & 3
    away = (((ze & 1) + c) & 1) * 16 + ((xe - x) & 3) * 4 + ((ye - y) & 3)
    slot_row = ((ze >> 1) * PEERS + away) * SLOT + rank_row
    diag = iota((ROUTES, ROUTES), 0) == iota((ROUTES, ROUTES), 1)
    slot_col = jnp.sum(jnp.where(diag, slot_row.astype(F32), 0.0), axis=1, keepdims=True).astype(I32)
    gcol = jnp.sum(jnp.where(diag, gate_row, 0.0), axis=1, keepdims=True)
    gcol_ref[...] = jnp.broadcast_to(gcol, (ROUTES, 128))

    at0 = iota((2 * ROWS, ROUTES), 0)
    rowsel[0] = pick(at0 == slot_row)
    for j in range(3):
        rowsel[1 + j] = pick((at0 % SLOT >= 12) & (at0 + (4 * j - 12) == slot_row))

    scaled = (hid_ref[...].astype(F32) * gcol).astype(BF)
    tail = scaled[:, CUT:]

    def packed(cols, extra):
        for q in range(2):
            rows = slice(q * ROWS, (q + 1) * ROWS)
            out = dot(rowsel[0, rows], scaled[:, cols])
            add = [dot(rowsel[1 + j, rows], tail) for j in extra]
            if len(add) == 2:
                out = out + jnp.concatenate(add, axis=1)
            elif len(add) == 1:
                out = out + jnp.concatenate([add[0], jnp.zeros((ROWS, 128), F32)], axis=1)
            pack[q, :, cols] = out.astype(BF)

    packed(slice(0, 256), (0, 1))
    packed(slice(256, 512), (2,))
    packed(slice(512, 640), ())

    def send_hid(j, carry):
        remote(pack.at[:, slot_rows(j)], got.at[:, slot_rows(j)], hid_s, hid_r, plane(j, 1)).start()
        return carry

    lax.fori_loop(1, PEERS, send_hid, 0)
    got[:, :SLOT, :] = pack[:, :SLOT, :]

    at1 = iota((ROUTES, 2 * ROWS), 1)
    colsel[0] = pick(at1 == slot_col)
    for j in range(3):
        colsel[1 + j] = pick((at1 % SLOT >= 12) & (at1 + (4 * j - 12) == slot_col))

    q_up = jnp.where(side, ((zb + 3) % 4) // 2, ((zb + 2) % 4) // 2)
    q_down = jnp.where(side, ((zb + 1) % 4) // 2, ((zb + 2) % 4) // 2)

    lag = jnp.where(side, 0, 4)
    streams = ((0, q_up, zl < 3, lag + zl), (1, q_down, zl > 0, lag + 3 - zl))

    def relay(step):
        for way, q, inner, late in streams:
            i = step - late
            first = i < CH // 2
            here = (i >= 0) & (i < jnp.where(side, CH, CH // 2))

            @pl.when(here)
            def _():
                w_copy(q, i, way).wait_recv()

            @pl.when(here & (inner | (side & first)))
            def _():
                w_copy(q, i, way).start()

    def relay_sent(i):
        first = i < CH // 2
        for way, q, inner, _ in streams:

            @pl.when((side & (inner | first)) | (home & (jnp.logical_not(inner) | first)))
            def _():
                w_copy(q, i, way).wait_send()

    def forward(j):
        remote(tok.at[pl.ds(0, TOK)], tok.at[slot_rows(j, TOK)], tok_s, tok_r.at[j], plane(j, 1)).wait_recv()
        remote(tok.at[slot_rows(j, TOK)], tok.at[slot_rows(j + 16, TOK)], fwd_s, fwd_r, partner).start()

    def early(i, carry):
        relay(i)

        @pl.when(i > 0)
        def _():
            forward(2 * i)

        forward(2 * i + 1)
        return carry

    lax.fori_loop(0, 8, early, 0)

    remote(meta.at[pl.ds(1, PEERS - 1)], meta.at[pl.ds(1, PEERS - 1)], meta_s, meta_r, partner).wait_recv()
    remote(tok.at[pl.ds(0, 16 * TOK)], tok.at[pl.ds(16 * TOK, 16 * TOK)], fwd_s, fwd_r, partner).wait_recv()

    block = pick((iota((256, 256), 0) < iota((256, 256), 1)) & (iota((256, 256), 0) // TOK == iota((256, 256), 1) // TOK))

    def gather(group):
        halves = []
        for half in range(2):
            first = group * 8 + half * 4
            total = meta[first, :TOP].astype(F32)
            for j in range(1, 4):
                total += meta[first + j, :TOP].astype(F32)
            halves.append(total)
        named = jnp.concatenate(halves, axis=1).astype(I32)
        hits = []
        for q in range(2):
            mine = x * 16 + (c + 2 * q) * 4 + y
            hits.append(jnp.sum(jnp.where(named == mine, 1.0, 0.0), axis=0, keepdims=True))
        both = jnp.concatenate(hits + [jnp.zeros((6, 256), F32)], axis=0)
        ranks = dot(both.astype(BF), block).astype(I32)
        sel = []
        for q in range(2):
            to = (iota((1, 256), 1) // TOK) * SLOT + ranks[q : q + 1, :]
            to = jnp.where(hits[q] > 0.5, to, -1)
            sel.append(pick(iota((128, 256), 0) == to))
        sel = jnp.concatenate(sel, axis=0)

        def columns(n, carry):
            cols = pl.ds(pl.multiple_of(n * 512, 512), 512)
            out = dot(sel, tok[group * 256 : (group + 1) * 256, cols]).astype(BF)
            g[0, group * 128 : (group + 1) * 128, cols] = out[:128]
            g[1, group * 128 : (group + 1) * 128, cols] = out[128:]
            return carry

        lax.fori_loop(0, D // 512, columns, 0)

    def turn(q):
        row = iota((ROWS, 128), 0) % SLOT
        last = jnp.zeros((ROWS, 128), F32)
        for j in range(3):
            moved = pltpu.roll(got[q, :, j * 128 : (j + 1) * 128].astype(F32), ROWS - 12 + 4 * j, 0)
            last = jnp.where(row // 4 == j, moved, last)
        for j in range(2):
            ht[q, j * 256 : (j + 1) * 256, :] = got[q, :, j * 256 : (j + 1) * 256].T
        ht[q, 512:640, :] = got[q, :, 512:640].T
        ht[q, 640:768, :] = last.astype(BF).T

    def outer(q):
        def columns(n, carry):
            cols = pl.ds(pl.multiple_of(n * 256, 256), 256)
            part[q, :, cols] = dot(ht[q], g[q, :, cols]).astype(BF)
            return carry

        lax.fori_loop(0, D // 256, columns, 0)

    def wait_hid():
        remote(
            got.at[:, pl.ds(SLOT, ROWS - SLOT)], got.at[:, pl.ds(SLOT, ROWS - SLOT)], hid_s, hid_r, partner
        ).wait_recv()

    pieces = [
        lambda: gather(0), lambda: gather(1), lambda: gather(2), lambda: gather(3),
        lambda: (wait_hid(), turn(0)), lambda: (outer(0), turn(1)), lambda: outer(1),
    ]
    for i in range(8, CH + 3):
        relay(i)
        if i - 8 < len(pieces):
            pieces[i - 8]()

    def mine(zd):
        return (zd // 4) % 2 == c

    def own(zd, k):
        return (zd // 4) // 2, pl.ds(pl.multiple_of((zd % 4) * SLAB + k * SR, SR), SR)

    def sub(k):
        return pl.ds(pl.multiple_of(k * SR, SR), SR)

    def hop(src, way, s, k):
        land, sem, to = (land_p, rs_rp, up) if way == 0 else (land_m, rs_rm, down)
        return remote(src, land.at[s, sub(k)], rs_s.at[way, s, k], sem.at[s, k], column(to))

    targets = ((0, lambda s: (z + 7 - s) % 16, 7), (1, lambda s: (z + 8 + s) % 16, 8))

    def launch(k, carry):
        for way, target, _ in targets:
            zd = target(0)

            @pl.when(mine(zd))
            def _():
                q, rows = own(zd, k)
                hop(part.at[q, rows], way, 0, k).start()

        return carry

    lax.fori_loop(0, SUB, launch, 0)

    def add_step(s):
        def body(k, carry):
            for way, target, count in targets:
                if s >= count:
                    continue
                zd = target(s)
                land = land_p if way == 0 else land_m

                @pl.when(mine(zd))
                def _():
                    q, rows = own(zd, k)
                    hop(land.at[s - 1, sub(k)], way, s - 1, k).wait_recv()
                    land[s - 1, sub(k), :] = (
                        land[s - 1, sub(k), :].astype(F32) + part[q, rows, :].astype(F32)
                    ).astype(BF)
                    hop(land.at[s - 1, sub(k)], way, s, k).start()

            return carry

        lax.fori_loop(0, SUB, body, 0)

    def project(q, tile):
        out = dot(g[q], wbuf[q, tile * 256 : (tile + 1) * 256, :], ((1,), (1,)))
        row = iota((ROWS, 128), 0) % SLOT
        if tile == 2:
            proj5[...] = out[:, 128:]
            cell[q, :, 512:640] = out[:, :128].astype(BF)
            return
        for n in range(2):
            j = tile * 2 + n
            part_out = out[:, n * 128 : (n + 1) * 128]
            if j < 3:
                part_out = jnp.where(row >= 12, pltpu.roll(proj5[...], 12 - 4 * j, 0), part_out)
            cell[q, :, j * 128 : (j + 1) * 128] = part_out.astype(BF)

    def send_back():
        def start(j, carry):
            remote(cell.at[:, slot_rows(j)], back.at[:, slot_rows(j)], ret_s, ret_r, plane(j, -1)).start()
            return carry

        lax.fori_loop(1, PEERS, start, 0)
        back[:, :SLOT, :] = cell[:, :SLOT, :]

    def finish():
        remote(
            back.at[:, pl.ds(SLOT, ROWS - SLOT)], back.at[:, pl.ds(SLOT, ROWS - SLOT)], ret_s, ret_r, partner
        ).wait_recv()
        gate = gcol_ref[:, :1]
        total = jnp.zeros((ROUTES, 1), F32)

        def routed(sel, cols):
            return dot(colsel[sel, :, :ROWS], back[0, :, cols]) + dot(colsel[sel, :, ROWS:], back[1, :, cols])

        for lo, hi in ((0, 256), (256, 512), (512, 640), (640, 768)):
            if lo < CUT:
                out = routed(0, slice(lo, hi))
            else:
                out = sum(routed(1 + j, slice(j * 128, (j + 1) * 128)) for j in range(3))
            hg_ref[:, lo:hi] = (gate * out).astype(BF)
            total += jnp.sum(out * hid_ref[:, lo:hi].astype(F32), axis=1, keepdims=True)
        spread = jnp.where(iota((ROUTES, TOP), 0) % TOP == iota((ROUTES, TOP), 1), total, 0.0)
        gg_ref[...] = jnp.sum(spread.reshape(TOK, TOP, TOP), axis=1)

    add_step(1)
    for tile in (2, 0, 1):
        project(0, tile)
    add_step(2)
    for tile in (2, 0, 1):
        project(1, tile)
    send_back()
    add_step(3)
    add_step(4)
    add_step(5)
    finish()
    add_step(6)
    add_step(7)

    @pl.when(mine(z))
    def _():
        def close(n, carry):
            k = jnp.where(n < 2, 2 * (1 - c) + n, 2 * c + n - 2)
            q, rows = own(z, k)
            hop(land_p.at[6, sub(k)], 0, 6, k).wait_recv()
            hop(land_m.at[7, sub(k)], 1, 7, k).wait_recv()
            out = (
                land_p[6, sub(k), :].astype(F32)
                + land_m[7, sub(k), :].astype(F32)
                + part[q, rows, :].astype(F32)
            )

            @pl.when(n < 2)
            def _():
                fin_out[sub(n % 2), :] = out.astype(BF)
                remote(fin_out.at[sub(n % 2)], fin_in.at[sub(n % 2)], fin_s.at[n % 2], fin_r.at[n % 2], partner).start()

            @pl.when(n >= 2)
            def _():
                wg_ref[sub(n % 2), :] = out

            return carry

        lax.fori_loop(0, SUB, close, 0)

        def sent(n, carry):
            remote(fin_out.at[sub(n)], fin_in.at[sub(n)], fin_s.at[n], fin_r.at[n], partner).wait_send()
            return carry

        lax.fori_loop(0, 2, sent, 0)

    @pl.when(jnp.logical_not(mine(z)))
    def _():
        def close(n, carry):
            remote(fin_out.at[sub(n)], fin_in.at[sub(n)], fin_s.at[n], fin_r.at[n], partner).wait_recv()
            wg_ref[sub(n), :] = fin_in[sub(n), :].astype(F32)
            return carry

        lax.fori_loop(0, 2, close, 0)

    remote(meta.at[pl.ds(1, PEERS - 1)], meta.at[pl.ds(1, PEERS - 1)], meta_s, meta_r, partner).wait_send()
    remote(tok.at[pl.ds(0, 16 * TOK)], tok.at[pl.ds(0, 16 * TOK)], tok_s, fwd_r, partner).wait_send()
    remote(tok.at[pl.ds(TOK, 15 * TOK)], tok.at[pl.ds(TOK, 15 * TOK)], fwd_s, fwd_r, partner).wait_send()
    remote(
        pack.at[:, pl.ds(SLOT, ROWS - SLOT)], got.at[:, pl.ds(SLOT, ROWS - SLOT)], hid_s, hid_r, partner
    ).wait_send()
    remote(
        cell.at[:, pl.ds(SLOT, ROWS - SLOT)], back.at[:, pl.ds(SLOT, ROWS - SLOT)], ret_s, ret_r, partner
    ).wait_send()

    def all_relayed(i, carry):
        relay_sent(i)
        return carry

    lax.fori_loop(0, CH, all_relayed, 0)

    def all_added(k, carry):
        for way, target, count in targets:
            for s in range(count):

                @pl.when(mine(target(s)))
                def _():
                    hop(land_m.at[0, sub(k)], way, s, k).wait_send()

        return carry

    lax.fori_loop(0, SUB, all_added, 0)


def on_device(grad_out, hidden, gates, routes, weights):
    tokens, picks = routes.shape
    vmem = pl.BlockSpec(memory_space=pltpu.VMEM)
    dma = pltpu.SemaphoreType.DMA
    hidden_grad, gate_grad, weight_grad = pl.pallas_call(
        kernel,
        out_shape=(
            jax.ShapeDtypeStruct((ROUTES, F), BF),
            jax.ShapeDtypeStruct((TOK, TOP), F32),
            jax.ShapeDtypeStruct((F // 8, D), F32),
        ),
        in_specs=[vmem, vmem, vmem, vmem, pl.BlockSpec(memory_space=pl.ANY)],
        out_specs=(vmem, vmem, vmem),
        scratch_shapes=[
            pltpu.VMEM((PEERS * TOK, D), BF),
            pltpu.VMEM((PEERS, 16, 128), BF),
            pltpu.VMEM((4, 16, 128), BF),
            pltpu.VMEM((2, ROWS, CUT), BF),
            pltpu.VMEM((2, ROWS, CUT), BF),
            pltpu.VMEM((2, ROWS, CUT), BF),
            pltpu.VMEM((2, ROWS, CUT), BF),
            pltpu.VMEM((4, 2 * ROWS, ROUTES), BF),
            pltpu.VMEM((4, ROUTES, 2 * ROWS), BF),
            pltpu.VMEM((ROUTES, 128), F32),
            pltpu.VMEM((2, F, D), BF),
            pltpu.VMEM((2, ROWS, D), BF),
            pltpu.VMEM((2, F, ROWS), BF),
            pltpu.VMEM((ROWS, 128), F32),
            pltpu.VMEM((2, F, D), BF),
            pltpu.VMEM((7, SLAB, D), BF),
            pltpu.VMEM((8, SLAB, D), BF),
            pltpu.VMEM((F // 8, D), BF),
            pltpu.VMEM((F // 8, D), BF),
            dma, dma, dma, dma, dma((16,)), dma, dma, dma, dma, dma, dma,
            dma((2, CH)), dma((2, CH)), dma((2, 8, SUB)), dma((7, SUB)), dma((8, SUB)),
            dma((2,)), dma((2,)),
        ],
        compiler_params=pltpu.CompilerParams(
            collective_id=0, has_side_effects=True, vmem_limit_bytes=60 * 2**20
        ),
        cost_estimate=pl.CostEstimate(flops=10**10, bytes_accessed=10**7, transcendentals=0),
        name="routed_down_backward",
    )(routes.T, gates.T, grad_out, hidden.reshape(ROUTES, F), weights.reshape(F, D))
    return (
        hidden_grad.reshape(tokens, picks, F),
        gate_grad,
        weight_grad.reshape(1, F // 8, D),
    )


def solution(mesh):
    return jax.shard_map(
        on_device,
        mesh=mesh,
        in_specs=(
            P(("dp", "expert"), None),
            P(("dp", "expert"), None, None),
            P(("dp", "expert"), None),
            P(("dp", "expert"), None),
            P("expert", None, None),
        ),
        out_specs=(
            P(("dp", "expert"), None, None),
            P(("dp", "expert"), None),
            P("expert", "dp", None),
        ),
        check_vma=False,
    )
```

time: 487 us -> 223 us (0.46)
  the two profiles are of different devices: /device:TPU:1 before, /device:TPU:99 now
where the time goes in v1:
time: 223 us
  Pallas kernels  217 us (97%)
  local copies, waits for them, and re-layouts  5.21 us (2%)
    pallas_call x1, Pallas kernels, on_device(): pl.pallas_call(kernel, out_shape=(jax.ShapeDtypeStruct((ROUTES, F), BF),...  217 us
    unnamed x3, local copies, waits for them, and re-layouts  5.21 us

profile of v1, /device:TPU:99, one launch (start us, length us, event | category | flops | bytes accessed | tf_op | source)
XLA Modules:
  0.0 223.1 jit_solution(15175139413224267025)
XLA Ops:
  0.6 217.3 %routed_down_backward.1 = (bf16[256,768]{1,0:T(8,128)(2,1)}, f32[32,8]{1,0:T(8,128)}, f32[96,2048]{1,0:T(8,128)}) custom-call(s32[8,32]{1,0:T(8,128)} %bitcast.10, bf16[8,32]{1,0:T(8,128)(2,1)} %bitcast.11, bf16[32,2048]{1,0:T(8,128)(2,1)} %grad_ref.1, bf16[256,768]{1,0:T(8,128)(2,1)} %bitcast.9, bf16[768,2048]{1,0:T(8,128)(2,1)} %bitcast.8), custom_call_target="tpu_custom_call" | custom-call | flops 10000000000 | bytes 10000000 | tf_op jit(solution)/shard_map/routed_down_backward/pallas_call | solution.py:497
  217.9 1.4 copy.8
  219.3 1.8 copy.11
  221.1 2.1 copy.12

commit v2 on v1

--- a/solution.py
+++ b/solution.py
@@ -21,11 +21,16 @@
 SLOT = 16
 PEERS = 32
 ROWS = PEERS * SLOT
-CH = 16
+CH = 24
 CR = F // CH
 SLAB = 192
-SUB = 4
+SUB = 6
+FIRST = 16
+SKEW = 2
+STEPS = max(CH + 3 * SKEW, CH // 2 + 7 * SKEW)
+AHEAD = 4
 SR = SLAB // SUB
+HALF = SUB // 2
 
 
 def iota(shape, dim):
@@ -105,20 +110,11 @@
         ).astype(BF)
     meta[0] = meta_out[0]
 
+    @pl.when(home)
+    def _():
+        pltpu.make_async_copy(w_ref, wbuf.at[own_q], w_sem).wait()
+
     pl.semaphore_wait(barrier, PEERS - 1 + 2)
-
-    def send_meta(j, carry):
-        remote(meta_out.at[j % 4], meta.at[j], meta_s, meta_r, plane(j, 1)).start()
-        return carry
-
-    lax.fori_loop(1, PEERS, send_meta, 0)
-
-    def send_tok(j, carry):
-        remote(tok.at[pl.ds(0, TOK)], tok.at[slot_rows(j, TOK)], tok_s, tok_r.at[j], plane(j, 1)).start()
-        return carry
-
-    lax.fori_loop(1, 16, send_tok, 0)
-    remote(tok.at[pl.ds(0, TOK)], tok.at[pl.ds(16 * TOK, TOK)], tok_s, fwd_r, partner).start()
 
     def w_rows(i):
         return pl.ds(pl.multiple_of(i * CR, CR), CR)
@@ -130,10 +126,6 @@
             rel_s.at[way, i], rel_r.at[way, i], column(up if way == 0 else down),
         )
 
-    @pl.when(home)
-    def _():
-        pltpu.make_async_copy(w_ref, wbuf.at[own_q], w_sem).wait()
-
     for way, edge in ((0, 3), (1, 0)):
 
         @pl.when(home & (zl == edge))
@@ -142,7 +134,20 @@
                 w_copy(own_q, i, way).start()
                 return carry
 
-            lax.fori_loop(0, CH, start, 0)
+            lax.fori_loop(0, AHEAD, start, 0)
+
+    def send_tok(j, carry):
+        remote(tok.at[pl.ds(0, TOK)], tok.at[slot_rows(j, TOK)], tok_s, tok_r.at[j], plane(j, 1)).start()
+        return carry
+
+    lax.fori_loop(1, 16, send_tok, 0)
+    remote(tok.at[pl.ds(0, TOK)], tok.at[pl.ds(16 * TOK, TOK)], tok_s, fwd_r, partner).start()
+
+    def send_meta(j, carry):
+        remote(meta_out.at[j % 4], meta.at[j], meta_s, meta_r, plane(j, 1)).start()
+        return carry
+
+    lax.fori_loop(1, PEERS, send_meta, 0)
 
     rt = routes.astype(BF)
     widen = pick(iota((TOK, ROUTES), 1) // TOP == iota((TOK, ROUTES), 0))
@@ -206,7 +211,7 @@
     q_down = jnp.where(side, ((zb + 1) % 4) // 2, ((zb + 2) % 4) // 2)
 
     lag = jnp.where(side, 0, 4)
-    streams = ((0, q_up, zl < 3, lag + zl), (1, q_down, zl > 0, lag + 3 - zl))
+    streams = ((0, q_up, zl < 3, SKEW * (lag + zl)), (1, q_down, zl > 0, SKEW * (lag + 3 - zl)))
 
     def relay(step):
         for way, q, inner, late in streams:
@@ -222,6 +227,10 @@
             def _():
                 w_copy(q, i, way).start()
 
+            @pl.when(home & jnp.logical_not(inner) & (step < CH - AHEAD))
+            def _():
+                w_copy(own_q, step + AHEAD, way).start()
+
     def relay_sent(i):
         first = i < CH // 2
         for way, q, inner, _ in streams:
@@ -234,20 +243,24 @@
         remote(tok.at[pl.ds(0, TOK)], tok.at[slot_rows(j, TOK)], tok_s, tok_r.at[j], plane(j, 1)).wait_recv()
         remote(tok.at[slot_rows(j, TOK)], tok.at[slot_rows(j + 16, TOK)], fwd_s, fwd_r, partner).start()
 
-    def early(i, carry):
+    def relay_only(i, carry):
         relay(i)
-
-        @pl.when(i > 0)
-        def _():
-            forward(2 * i)
-
-        forward(2 * i + 1)
-        return carry
-
-    lax.fori_loop(0, 8, early, 0)
-
-    remote(meta.at[pl.ds(1, PEERS - 1)], meta.at[pl.ds(1, PEERS - 1)], meta_s, meta_r, partner).wait_recv()
-    remote(tok.at[pl.ds(0, 16 * TOK)], tok.at[pl.ds(16 * TOK, 16 * TOK)], fwd_s, fwd_r, partner).wait_recv()
+        return carry
+
+    lax.fori_loop(0, FIRST, relay_only, 0)
+
+    def wait_meta():
+        remote(meta.at[pl.ds(1, PEERS - 1)], meta.at[pl.ds(1, PEERS - 1)], meta_s, meta_r, partner).wait_recv()
+
+    def wait_partner():
+        remote(tok.at[pl.ds(0, 16 * TOK)], tok.at[pl.ds(16 * TOK, 16 * TOK)], fwd_s, fwd_r, partner).wait_recv()
+
+    def forwards(lo, hi):
+        def body(j, carry):
+            forward(j)
+            return carry
+
+        lax.fori_loop(lo, hi, body, 0)
 
     block = pick((iota((256, 256), 0) < iota((256, 256), 1)) & (iota((256, 256), 0) // TOK == iota((256, 256), 1) // TOK))
 
@@ -307,13 +320,15 @@
         ).wait_recv()
 
     pieces = [
-        lambda: gather(0), lambda: gather(1), lambda: gather(2), lambda: gather(3),
-        lambda: (wait_hid(), turn(0)), lambda: (outer(0), turn(1)), lambda: outer(1),
+        lambda: forwards(1, 8), lambda: forwards(8, 16),
+        lambda: (wait_meta(), gather(0)), lambda: gather(1),
+        lambda: (wait_hid(), turn(0)), lambda: turn(1),
+        lambda: (wait_partner(), gather(2)), lambda: gather(3),
+        lambda: outer(0), lambda: outer(1),
     ]
-    for i in range(8, CH + 3):
-        relay(i)
-        if i - 8 < len(pieces):
-            pieces[i - 8]()
+    for i, piece in enumerate(pieces):
+        relay(FIRST + i)
+        piece()
 
     def mine(zd):
         return (zd // 4) % 2 == c
@@ -328,30 +343,33 @@
         land, sem, to = (land_p, rs_rp, up) if way == 0 else (land_m, rs_rm, down)
         return remote(src, land.at[s, sub(k)], rs_s.at[way, s, k], sem.at[s, k], column(to))
 
-    targets = ((0, lambda s: (z + 7 - s) % 16, 7), (1, lambda s: (z + 8 + s) % 16, 8))
+    targets = ((0, lambda s: (z + 8 - s) % 16), (1, lambda s: (z + 8 + s) % 16))
+
+    def far(way, k):
+        return k >= HALF if way == 0 else k < HALF
 
     def launch(k, carry):
-        for way, target, _ in targets:
-            zd = target(0)
-
-            @pl.when(mine(zd))
-            def _():
-                q, rows = own(zd, k)
-                hop(part.at[q, rows], way, 0, k).start()
+        for way, target in targets:
+            for s in range(2):
+                zd = target(s)
+
+                @pl.when(mine(zd) & (far(way, k) if s == 0 else jnp.logical_not(far(way, k))))
+                def _():
+                    q, rows = own(zd, k)
+                    hop(part.at[q, rows], way, s, k).start()
 
         return carry
 
     lax.fori_loop(0, SUB, launch, 0)
+    lax.fori_loop(FIRST + len(pieces), STEPS, relay_only, 0)
 
     def add_step(s):
         def body(k, carry):
-            for way, target, count in targets:
-                if s >= count:
-                    continue
+            for way, target in targets:
                 zd = target(s)
                 land = land_p if way == 0 else land_m
 
-                @pl.when(mine(zd))
+                @pl.when(mine(zd) & (far(way, k) | (s > 1)))
                 def _():
                     q, rows = own(zd, k)
                     hop(land.at[s - 1, sub(k)], way, s - 1, k).wait_recv()
@@ -423,24 +441,24 @@
     @pl.when(mine(z))
     def _():
         def close(n, carry):
-            k = jnp.where(n < 2, 2 * (1 - c) + n, 2 * c + n - 2)
+            k = jnp.where(n < HALF, HALF * (1 - c) + n, HALF * c + n - HALF)
             q, rows = own(z, k)
-            hop(land_p.at[6, sub(k)], 0, 6, k).wait_recv()
+            hop(land_p.at[7, sub(k)], 0, 7, k).wait_recv()
             hop(land_m.at[7, sub(k)], 1, 7, k).wait_recv()
             out = (
-                land_p[6, sub(k), :].astype(F32)
+                land_p[7, sub(k), :].astype(F32)
                 + land_m[7, sub(k), :].astype(F32)
                 + part[q, rows, :].astype(F32)
             )
 
-            @pl.when(n < 2)
+            @pl.when(n < HALF)
             def _():
-                fin_out[sub(n % 2), :] = out.astype(BF)
-                remote(fin_out.at[sub(n % 2)], fin_in.at[sub(n % 2)], fin_s.at[n % 2], fin_r.at[n % 2], partner).start()
-
-            @pl.when(n >= 2)
+                fin_out[sub(n % HALF), :] = out.astype(BF)
+                remote(fin_out.at[sub(n % HALF)], fin_in.at[sub(n % HALF)], fin_s.at[n % HALF], fin_r.at[n % HALF], partner).start()
+
+            @pl.when(n >= HALF)
             def _():
-                wg_ref[sub(n % 2), :] = out
+                wg_ref[sub(n % HALF), :] = out
 
             return carry
 
@@ -450,7 +468,7 @@
             remote(fin_out.at[sub(n)], fin_in.at[sub(n)], fin_s.at[n], fin_r.at[n], partner).wait_send()
             return carry
 
-        lax.fori_loop(0, 2, sent, 0)
+        lax.fori_loop(0, HALF, sent, 0)
 
     @pl.when(jnp.logical_not(mine(z)))
     def _():
@@ -459,7 +477,7 @@
             wg_ref[sub(n), :] = fin_in[sub(n), :].astype(F32)
             return carry
 
-        lax.fori_loop(0, 2, close, 0)
+        lax.fori_loop(0, HALF, close, 0)
 
     remote(meta.at[pl.ds(1, PEERS - 1)], meta.at[pl.ds(1, PEERS - 1)], meta_s, meta_r, partner).wait_send()
     remote(tok.at[pl.ds(0, 16 * TOK)], tok.at[pl.ds(0, 16 * TOK)], tok_s, fwd_r, partner).wait_send()
@@ -478,10 +496,10 @@
     lax.fori_loop(0, CH, all_relayed, 0)
 
     def all_added(k, carry):
-        for way, target, count in targets:
-            for s in range(count):
-
-                @pl.when(mine(target(s)))
+        for way, target in targets:
+            for s in range(8):
+
+                @pl.when(mine(target(s)) & (far(way, k) | (s > 0)))
                 def _():
                     hop(land_m.at[0, sub(k)], way, s, k).wait_send()
 
@@ -519,13 +537,13 @@
             pltpu.VMEM((2, F, ROWS), BF),
             pltpu.VMEM((ROWS, 128), F32),
             pltpu.VMEM((2, F, D), BF),
-            pltpu.VMEM((7, SLAB, D), BF),
+            pltpu.VMEM((8, SLAB, D), BF),
             pltpu.VMEM((8, SLAB, D), BF),
             pltpu.VMEM((F // 8, D), BF),
             pltpu.VMEM((F // 8, D), BF),
             dma, dma, dma, dma, dma((16,)), dma, dma, dma, dma, dma, dma,
-            dma((2, CH)), dma((2, CH)), dma((2, 8, SUB)), dma((7, SUB)), dma((8, SUB)),
-            dma((2,)), dma((2,)),
+            dma((2, CH)), dma((2, CH)), dma((2, 8, SUB)), dma((8, SUB)), dma((8, SUB)),
+            dma((HALF,)), dma((HALF,)),
         ],
         compiler_params=pltpu.CompilerParams(
             collective_id=0, has_side_effects=True, vmem_limit_bytes=60 * 2**20

time: 223 us -> 172 us (0.77)
  the two profiles are of different devices: /device:TPU:99 before, /device:TPU:1 now
where the time goes in v2:
time: 172 us
  Pallas kernels  166 us (97%)
  local copies, waits for them, and re-layouts  5.21 us (3%)
    pallas_call x1, Pallas kernels, on_device(): pl.pallas_call(kernel, out_shape=(jax.ShapeDtypeStruct((ROUTES, F), BF),...  166 us
    unnamed x3, local copies, waits for them, and re-layouts  5.21 us

profile of v2, /device:TPU:1, one launch (start us, length us, event | category | flops | bytes accessed | tf_op | source)
XLA Modules:
  0.0 172.0 jit_solution(11561323332504474766)
XLA Ops:
  0.6 166.1 %routed_down_backward.1 = (bf16[256,768]{1,0:T(8,128)(2,1)}, f32[32,8]{1,0:T(8,128)}, f32[96,2048]{1,0:T(8,128)}) custom-call(s32[8,32]{1,0:T(8,128)} %bitcast.10, bf16[8,32]{1,0:T(8,128)(2,1)} %bitcast.11, bf16[32,2048]{1,0:T(8,128)(2,1)} %grad_ref.1, bf16[256,768]{1,0:T(8,128)(2,1)} %bitcast.9, bf16[768,2048]{1,0:T(8,128)(2,1)} %bitcast.8), custom_call_target="tpu_custom_call" | custom-call | flops 10000000000 | bytes 10000000 | tf_op jit(solution)/shard_map/routed_down_backward/pallas_call | solution.py:515
  166.8 1.4 copy.8
  168.1 1.8 %copy.11 = bf16[32,8,768]{2,1,0:T(8,128)(2,1)} copy(bf16[32,8,768]{2,1,0:T(8,128)(2,1)} %bitcast.7) | data formatting | bytes 786432
  169.9 2.1 %copy.12 = f32[1,96,2048]{2,1,0:T(8,128)} copy(f32[1,96,2048]{2,1,0:T(8,128)} %bitcast.6) | data formatting | bytes 1572864

commit v3 on v2

--- a/solution.py
+++ b/solution.py
@@ -21,14 +21,17 @@
 SLOT = 16
 PEERS = 32
 ROWS = PEERS * SLOT
-CH = 24
+CH = 48
 CR = F // CH
 SLAB = 192
 SUB = 6
-FIRST = 16
-SKEW = 2
+TURN = 8
+FIRST = 32
+SKEW = 4
+PER = 3
+RATE = 1
 STEPS = max(CH + 3 * SKEW, CH // 2 + 7 * SKEW)
-AHEAD = 4
+AHEAD = 8
 SR = SLAB // SUB
 HALF = SUB // 2
 
@@ -84,13 +87,14 @@
 
     barrier = pltpu.get_barrier_semaphore()
 
+    pl.semaphore_signal(barrier, inc=1, device_id=column(up), device_id_type=MESH)
+    pl.semaphore_signal(barrier, inc=1, device_id=column(down), device_id_type=MESH)
+
     def greet(j, carry):
         pl.semaphore_signal(barrier, inc=1, device_id=plane(j, 1), device_id_type=MESH)
         return carry
 
     lax.fori_loop(1, PEERS, greet, 0)
-    pl.semaphore_signal(barrier, inc=1, device_id=column(up), device_id_type=MESH)
-    pl.semaphore_signal(barrier, inc=1, device_id=column(down), device_id_type=MESH)
 
     own_q = zb // 2
 
@@ -98,7 +102,37 @@
     def _():
         pltpu.make_async_copy(w_ref, wbuf.at[own_q], w_sem).start()
 
+    @pl.when(home)
+    def _():
+        pltpu.make_async_copy(w_ref, wbuf.at[own_q], w_sem).wait()
+
+    pl.semaphore_wait(barrier, PEERS - 1 + 2)
+
+    def w_rows(i):
+        return pl.ds(pl.multiple_of(i * CR, CR), CR)
+
+    def w_copy(q, i, way):
+        chunk = i if way == 0 else CH - 1 - i
+        return remote(
+            wbuf.at[q, w_rows(chunk)], wbuf.at[q, w_rows(chunk)],
+            rel_s.at[way, i], rel_r.at[way, i], column(up if way == 0 else down),
+        )
+
+    for way, edge in ((0, 3), (1, 0)):
+
+        @pl.when(home & (zl == edge))
+        def _():
+            def start(i, carry):
+                w_copy(own_q, i, way).start()
+                return carry
+
+            lax.fori_loop(0, AHEAD, start, 0)
+
     tok[pl.ds(0, TOK), :] = grad_ref[...]
+
+    for j in (4, 12, 1, 3, 8, 2):
+        remote(tok.at[pl.ds(0, TOK)], tok.at[pl.ds(j * TOK, TOK)], tok_s, tok_r.at[j], plane(j, 1)).start()
+    remote(tok.at[pl.ds(0, TOK)], tok.at[pl.ds(16 * TOK, TOK)], tok_s, fwd_r, partner).start()
 
     routes = routes_ref[...].astype(F32)
     shifted = dot(
@@ -109,39 +143,6 @@
             [shifted[:, v * 128 : (v + 1) * 128], jnp.zeros((8, 128), F32)], axis=0
         ).astype(BF)
     meta[0] = meta_out[0]
-
-    @pl.when(home)
-    def _():
-        pltpu.make_async_copy(w_ref, wbuf.at[own_q], w_sem).wait()
-
-    pl.semaphore_wait(barrier, PEERS - 1 + 2)
-
-    def w_rows(i):
-        return pl.ds(pl.multiple_of(i * CR, CR), CR)
-
-    def w_copy(q, i, way):
-        chunk = i if way == 0 else CH - 1 - i
-        return remote(
-            wbuf.at[q, w_rows(chunk)], wbuf.at[q, w_rows(chunk)],
-            rel_s.at[way, i], rel_r.at[way, i], column(up if way == 0 else down),
-        )
-
-    for way, edge in ((0, 3), (1, 0)):
-
-        @pl.when(home & (zl == edge))
-        def _():
-            def start(i, carry):
-                w_copy(own_q, i, way).start()
-                return carry
-
-            lax.fori_loop(0, AHEAD, start, 0)
-
-    def send_tok(j, carry):
-        remote(tok.at[pl.ds(0, TOK)], tok.at[slot_rows(j, TOK)], tok_s, tok_r.at[j], plane(j, 1)).start()
-        return carry
-
-    lax.fori_loop(1, 16, send_tok, 0)
-    remote(tok.at[pl.ds(0, TOK)], tok.at[pl.ds(16 * TOK, TOK)], tok_s, fwd_r, partner).start()
 
     def send_meta(j, carry):
         remote(meta_out.at[j % 4], meta.at[j], meta_s, meta_r, plane(j, 1)).start()
@@ -239,15 +240,39 @@
             def _():
                 w_copy(q, i, way).wait_send()
 
+    def tok_wait(j):
+        remote(tok.at[pl.ds(0, TOK)], tok.at[slot_rows(j, TOK)], tok_s, tok_r.at[j], plane(j, 1)).wait_recv()
+
+    def turn_tokens():
+        for n in range(1, 4):
+            tok_wait(n)
+            tok_wait(4 * n)
+
+        def start(n, carry):
+            dx, dy = 1 + n // 3, 1 + n % 3
+            j = 4 * dx + dy
+            for half, start_at, to in ((0, 4 * dx, dy), (1, dy, 4 * dx)):
+                src = pl.ds(pl.multiple_of(start_at * TOK + half * 16, 16), 16)
+                dst = pl.ds(pl.multiple_of(j * TOK + half * 16, 16), 16)
+                remote(tok.at[src], tok.at[dst], tok_s, tok_r.at[j], plane(to, 1)).start()
+            return carry
+
+        lax.fori_loop(0, 9, start, 0)
+
     def forward(j):
-        remote(tok.at[pl.ds(0, TOK)], tok.at[slot_rows(j, TOK)], tok_s, tok_r.at[j], plane(j, 1)).wait_recv()
+        @pl.when((j > 4) & (j % 4 != 0))
+        def _():
+            tok_wait(j)
+
         remote(tok.at[slot_rows(j, TOK)], tok.at[slot_rows(j + 16, TOK)], fwd_s, fwd_r, partner).start()
 
     def relay_only(i, carry):
         relay(i)
         return carry
 
-    lax.fori_loop(0, FIRST, relay_only, 0)
+    lax.fori_loop(0, TURN, relay_only, 0)
+    turn_tokens()
+    lax.fori_loop(TURN, FIRST, relay_only, 0)
 
     def wait_meta():
         remote(meta.at[pl.ds(1, PEERS - 1)], meta.at[pl.ds(1, PEERS - 1)], meta_s, meta_r, partner).wait_recv()
@@ -320,14 +345,16 @@
         ).wait_recv()
 
     pieces = [
-        lambda: forwards(1, 8), lambda: forwards(8, 16),
-        lambda: (wait_meta(), gather(0)), lambda: gather(1),
-        lambda: (wait_hid(), turn(0)), lambda: turn(1),
-        lambda: (wait_partner(), gather(2)), lambda: gather(3),
-        lambda: outer(0), lambda: outer(1),
+        lambda: forwards(1, 16),
+        lambda: (wait_meta(), gather(0), gather(1)),
+        lambda: (wait_hid(), turn(0), turn(1)),
+        lambda: (wait_partner(), gather(2), gather(3)),
+        lambda: outer(0),
+        lambda: outer(1),
     ]
     for i, piece in enumerate(pieces):
-        relay(FIRST + i)
+        for n in range(PER):
+            relay(FIRST + i * PER + n)
         piece()
 
     def mine(zd):
@@ -361,26 +388,38 @@
         return carry
 
     lax.fori_loop(0, SUB, launch, 0)
-    lax.fori_loop(FIRST + len(pieces), STEPS, relay_only, 0)
-
-    def add_step(s):
-        def body(k, carry):
-            for way, target in targets:
-                zd = target(s)
-                land = land_p if way == 0 else land_m
-
-                @pl.when(mine(zd) & (far(way, k) | (s > 1)))
-                def _():
-                    q, rows = own(zd, k)
-                    hop(land.at[s - 1, sub(k)], way, s - 1, k).wait_recv()
-                    land[s - 1, sub(k), :] = (
-                        land[s - 1, sub(k), :].astype(F32) + part[q, rows, :].astype(F32)
-                    ).astype(BF)
-                    hop(land.at[s - 1, sub(k)], way, s, k).start()
-
-            return carry
-
-        lax.fori_loop(0, SUB, body, 0)
+    def add_sub(n):
+        s, k = 1 + n // SUB, n % SUB
+        for way, target in targets:
+            zd = target(s)
+            land = land_p if way == 0 else land_m
+
+            @pl.when(mine(zd) & (far(way, k) | (s > 1)))
+            def _():
+                q, rows = own(zd, k)
+                hop(land.at[s - 1, sub(k)], way, s - 1, k).wait_recv()
+                land[s - 1, sub(k), :] = (
+                    land[s - 1, sub(k), :].astype(F32) + part[q, rows, :].astype(F32)
+                ).astype(BF)
+                hop(land.at[s - 1, sub(k)], way, s, k).start()
+
+    def adds(lo, hi):
+        def body(n, carry):
+            add_sub(n)
+            return carry
+
+        lax.fori_loop(lo, hi, body, 0)
+
+    last = FIRST + len(pieces) * PER
+
+    def both(i, carry):
+        relay(i)
+        for r in range(RATE):
+            add_sub((i - last) * RATE + r)
+        return carry
+
+    lax.fori_loop(last, STEPS, both, 0)
+    done = (STEPS - last) * RATE
 
     def project(q, tile):
         out = dot(g[q], wbuf[q, tile * 256 : (tile + 1) * 256, :], ((1,), (1,)))
@@ -421,22 +460,20 @@
                 out = sum(routed(1 + j, slice(j * 128, (j + 1) * 128)) for j in range(3))
             hg_ref[:, lo:hi] = (gate * out).astype(BF)
             total += jnp.sum(out * hid_ref[:, lo:hi].astype(F32), axis=1, keepdims=True)
-        spread = jnp.where(iota((ROUTES, TOP), 0) % TOP == iota((ROUTES, TOP), 1), total, 0.0)
-        gg_ref[...] = jnp.sum(spread.reshape(TOK, TOP, TOP), axis=1)
-
-    add_step(1)
+        spread = jnp.where(iota((ROUTES, TOK), 0) // TOP == iota((ROUTES, TOK), 1), total, 0.0)
+        gg_ref[...] = jnp.sum(spread.reshape(TOK, TOP, TOK), axis=0)
+
+    marks = [done, done + SUB, done + 2 * SUB, 5 * SUB, 7 * SUB]
+    adds(marks[0], marks[1])
     for tile in (2, 0, 1):
         project(0, tile)
-    add_step(2)
+    adds(marks[1], marks[2])
     for tile in (2, 0, 1):
         project(1, tile)
     send_back()
-    add_step(3)
-    add_step(4)
-    add_step(5)
+    adds(marks[2], marks[3])
     finish()
-    add_step(6)
-    add_step(7)
+    adds(marks[3], marks[4])
 
     @pl.when(mine(z))
     def _():
@@ -508,15 +545,28 @@
     lax.fori_loop(0, SUB, all_added, 0)
 
 
+def settle(*refs):
+    held, sems = refs[6:9], refs[9]
+    into = [pltpu.make_async_copy(refs[i], held[i], sems.at[0, i]) for i in range(3)]
+    out = [pltpu.make_async_copy(held[i], refs[3 + i], sems.at[1, i]) for i in range(3)]
+    for copy in into:
+        copy.start()
+    for i in range(3):
+        into[i].wait()
+        out[i].start()
+    for copy in out:
+        copy.wait()
+
+
 def on_device(grad_out, hidden, gates, routes, weights):
     tokens, picks = routes.shape
     vmem = pl.BlockSpec(memory_space=pltpu.VMEM)
     dma = pltpu.SemaphoreType.DMA
-    hidden_grad, gate_grad, weight_grad = pl.pallas_call(
+    results = pl.pallas_call(
         kernel,
         out_shape=(
             jax.ShapeDtypeStruct((ROUTES, F), BF),
-            jax.ShapeDtypeStruct((TOK, TOP), F32),
+            jax.ShapeDtypeStruct((TOP, TOK), F32),
             jax.ShapeDtypeStruct((F // 8, D), F32),
         ),
         in_specs=[vmem, vmem, vmem, vmem, pl.BlockSpec(memory_space=pl.ANY)],
@@ -551,9 +601,18 @@
         cost_estimate=pl.CostEstimate(flops=10**10, bytes_accessed=10**7, transcendentals=0),
         name="routed_down_backward",
     )(routes.T, gates.T, grad_out, hidden.reshape(ROUTES, F), weights.reshape(F, D))
+    anywhere = pl.BlockSpec(memory_space=pl.ANY)
+    hidden_grad, gate_grad, weight_grad = pl.pallas_call(
+        settle,
+        out_shape=tuple(jax.ShapeDtypeStruct(r.shape, r.dtype) for r in results),
+        in_specs=[anywhere] * 3,
+        out_specs=(anywhere,) * 3,
+        scratch_shapes=[*(pltpu.VMEM(r.shape, r.dtype) for r in results), dma((2, 3))],
+        name="settle_results",
+    )(*results)
     return (
         hidden_grad.reshape(tokens, picks, F),
-        gate_grad,
+        gate_grad.T,
         weight_grad.reshape(1, F // 8, D),
     )
 

time: 172 us -> 163 us (0.948)
  local copies, waits for them, and re-layouts: 5.21 us -> 0 us
  Pallas kernels: 166 us -> 162 us
    pallas_call x1, Pallas kernels: 166 us -> 159 us  [on_device(): pl.pallas_call(kernel, out_shape=(jax.ShapeDtypeStruct((ROUTES, F), BF),...]
    unnamed x3 -> x0, local copies, waits for them, and re-layouts: 5.21 us -> none
    pallas_call x0 -> x1, Pallas kernels: none -> 2.19 us  [on_device(): pl.pallas_call(settle, out_shape=tuple((jax.ShapeDtypeStruct(r.shape, r.d...]
where the time goes in v3:
time: 163 us; the launch traced here: 162 us
  Pallas kernels  162 us (99%)
    pallas_call x1, Pallas kernels, on_device(): pl.pallas_call(kernel, out_shape=(jax.ShapeDtypeStruct((ROUTES, F), BF),...  159 us

profile of v3, /device:TPU:1, one launch (start us, length us, event | category | flops | bytes accessed | tf_op | source)
XLA Modules:
  0.0 162.3 jit_solution(16803379240980118251)
XLA Ops:
  0.6 159.4 %routed_down_backward.1 = (bf16[256,768]{1,0:T(8,128)(2,1)}, f32[8,32]{1,0:T(8,128)}, f32[96,2048]{1,0:T(8,128)}) custom-call(s32[8,32]{1,0:T(8,128)} %bitcast.11, bf16[8,32]{1,0:T(8,128)(2,1)} %bitcast.13, bf16[32,2048]{1,0:T(8,128)(2,1)} %grad_ref.1, bf16[256,768]{1,0:T(8,128)(2,1)} %bitcast.9, bf16[768,2048]{1,0:T(8,128)(2,1)} %bitcast.7), custom_call_target="tpu_custom_call" | custom-call | flops 10000000000 | bytes 10000000 | tf_op jit(solution)/shard_map/routed_down_backward/pallas_call | solution.py:565
  160.1 2.2 %settle_results.1 = (bf16[256,768]{1,0:T(8,128)(2,1)}, f32[8,32]{1,0:T(8,128)}, f32[96,2048]{1,0:T(8,128)}) custom-call(bf16[256,768]{1,0:T(8,128)(2,1)} %get-tuple-element.9.refs_0_, f32[8,32]{1,0:T(8,128)} %get-tuple-element.10.refs_1_, f32[96,2048]{1,0:T(8,128)} %get-tuple-element.11.refs_2_), custom_call_target="tpu_custom_call" | custom-call | tf_op jit(solution)/shard_map/settle_results/pallas_call | solution.py:605

commit v4 on v3

--- a/solution.py
+++ b/solution.py
@@ -25,7 +25,7 @@
 CR = F // CH
 SLAB = 192
 SUB = 6
-TURN = 8
+TURN = 10
 FIRST = 32
 SKEW = 4
 PER = 3
@@ -478,7 +478,8 @@
     @pl.when(mine(z))
     def _():
         def close(n, carry):
-            k = jnp.where(n < HALF, HALF * (1 - c) + n, HALF * c + n - HALF)
+            k = n
+            kept = n // HALF == c
             q, rows = own(z, k)
             hop(land_p.at[7, sub(k)], 0, 7, k).wait_recv()
             hop(land_m.at[7, sub(k)], 1, 7, k).wait_recv()
@@ -488,12 +489,12 @@
                 + part[q, rows, :].astype(F32)
             )
 
-            @pl.when(n < HALF)
+            @pl.when(jnp.logical_not(kept))
             def _():
                 fin_out[sub(n % HALF), :] = out.astype(BF)
                 remote(fin_out.at[sub(n % HALF)], fin_in.at[sub(n % HALF)], fin_s.at[n % HALF], fin_r.at[n % HALF], partner).start()
 
-            @pl.when(n >= HALF)
+            @pl.when(kept)
             def _():
                 wg_ref[sub(n % HALF), :] = out
 

time: 163 us -> 163 us (level)
  no operation moved by 1% of the time
where the time goes in v4:
time: 163 us; the launch traced here: 162 us
  Pallas kernels  162 us (99%)
    pallas_call x1, Pallas kernels, on_device(): pl.pallas_call(kernel, out_shape=(jax.ShapeDtypeStruct((ROUTES, F), BF),...  159 us

profile of v4, /device:TPU:1, one launch (start us, length us, event | category | flops | bytes accessed | tf_op | source)
XLA Modules:
  0.0 162.3 jit_solution(5301318626335158623)
XLA Ops:
  0.6 159.4 %routed_down_backward.1 = (bf16[256,768]{1,0:T(8,128)(2,1)}, f32[8,32]{1,0:T(8,128)}, f32[96,2048]{1,0:T(8,128)}) custom-call(s32[8,32]{1,0:T(8,128)} %bitcast.11, bf16[8,32]{1,0:T(8,128)(2,1)} %bitcast.13, bf16[32,2048]{1,0:T(8,128)(2,1)} %grad_ref.1, bf16[256,768]{1,0:T(8,128)(2,1)} %bitcast.9, bf16[768,2048]{1,0:T(8,128)(2,1)} %bitcast.7), custom_call_target="tpu_custom_call" | custom-call | flops 10000000000 | bytes 10000000 | tf_op jit(solution)/shard_map/routed_down_backward/pallas_call | solution.py:566
  160.1 2.2 %settle_results.1 = (bf16[256,768]{1,0:T(8,128)(2,1)}, f32[8,32]{1,0:T(8,128)}, f32[96,2048]{1,0:T(8,128)}) custom-call(bf16[256,768]{1,0:T(8,128)(2,1)} %get-tuple-element.9.refs_0_, f32[8,32]{1,0:T(8,128)} %get-tuple-element.10.refs_1_, f32[96,2048]{1,0:T(8,128)} %get-tuple-element.11.refs_2_), custom_call_target="tpu_custom_call" | custom-call | tf_op jit(solution)/shard_map/settle_results/pallas_call | solution.py:606
